TPU v7x, 32 devices: a whole 2x2x4 slice. The times are simulated.
32 devices in a mesh: section: 8 (over z, x), neuron: 4 (over y, core).
Axes of the slice: x: 2, y: 2, z: 4, core: 2. Of those that a mesh axis runs over, the one named last changes fastest.
Arguments:
- inputs: bfloat16 [6, 32768], P(None, 'neuron'), may hold values from 0 to 2
- weight_tiles: bfloat16 [8, 2048, 128, 128], P('section', 'neuron'), may hold values from -0.07324219 to 0.07910156
- source_block: int32 [8, 2048], P('section', 'neuron'), may hold values from 0 to 255
- target_block: int32 [8, 2048], P('section', 'neuron'), may hold values from 0 to 63
- live_slots: int32 [8, 4], P('section', 'neuron'), may hold values from 64 to 512, as said below
Outputs:
- activations: bfloat16 [8, 6, 32768], P('section', None, 'neuron')
Inputs may be any that keep to these rules, and one draw needn't show every extreme that they name: live_slots[l, n] is 512, 256, 128 or 64, and in every layer some shard has all 512 slots live.
All inputs are finite; a program needn't handle non-finite values.
Results may differ from a plain program's by a relative error of at most 0.0045.
Values may be sent and summed in bfloat16 or wider, within the bound.
A program may use at most 64 MiB of HBM per device.

v0:
```python
import jax
import jax.numpy as jnp
from jax import lax
from jax.sharding import PartitionSpec as P

NEURON_BIAS = -0.3
CLIP_LEVEL = 32.0


def from_behind(block, axis, distance):
    devices = range(lax.axis_size(axis))
    route = [(i - distance, i) for i in devices if i - distance in devices]
    return lax.ppermute(block, axis, route)


def layer_apply(gathered, weight_tiles, source_block, target_block, live_slots, column_count):
    row_count = gathered.shape[0]
    slot_count = weight_tiles.shape[1]
    block_size = weight_tiles.shape[2]
    block_count = gathered.shape[1] // block_size
    shaped = gathered.reshape(row_count, block_count, block_size)
    picked = jnp.take(shaped, source_block[0], axis=1)
    partial_value = jnp.einsum(
        "msk,skj->msj", picked, weight_tiles[0], preferred_element_type=jnp.float32
    )
    live_mask = jnp.arange(slot_count, dtype=jnp.int32) < live_slots[0, 0]
    selector = (
        target_block[0][:, None] == jnp.arange(column_count, dtype=jnp.int32)[None, :]
    ) & live_mask[:, None]
    summed = jnp.einsum(
        "msj,sc->mcj", partial_value, selector.astype(jnp.float32), precision=lax.Precision.HIGHEST
    )
    result = jnp.clip(summed + NEURON_BIAS, 0.0, CLIP_LEVEL).astype(jnp.bfloat16)
    return result.reshape(row_count, column_count * block_size)


def local(inputs, weight_tiles, source_block, target_block, live_slots):
    section_pos = lax.axis_index("section")
    section_count = lax.axis_size("section")
    total_rows = inputs.shape[0]
    shard_width = inputs.shape[1]
    column_count = shard_width // weight_tiles.shape[2]
    group_count = 1
    group_rows = total_rows // group_count
    step_count = section_count + group_count - 1

    def compute_layer(gathered):
        return layer_apply(
            gathered, weight_tiles, source_block, target_block, live_slots, column_count
        )

    def empty_layer(gathered):
        return jnp.zeros((group_rows, shard_width), jnp.bfloat16)

    def store_rows(collected, result, active):
        return jnp.where(active, result, collected)

    collected = jnp.zeros((total_rows, shard_width), jnp.bfloat16)

    def advance(step_num, state_pair):
        current_in, collected = state_pair
        micro_index = step_num - section_pos
        active = (micro_index >= 0) & (micro_index < group_count)
        gathered = lax.all_gather(current_in, "neuron", axis=1, tiled=True)
        result = lax.cond(active, compute_layer, empty_layer, gathered)
        collected = store_rows(collected, result, active)
        shifted = from_behind(result, "section", 1)
        current_in = jnp.where(section_pos == 0, inputs, shifted)
        return (current_in, collected)

    final_in, collected = lax.fori_loop(0, step_count, advance, (inputs, collected))
    return collected[None]


def solution(mesh):
    in_specs = (
        P(None, "neuron"),
        P("section", "neuron", None, None),
        P("section", "neuron"),
        P("section", "neuron"),
        P("section", "neuron"),
    )
    out_specs = P("section", None, "neuron")
    return jax.shard_map(local, mesh=mesh, in_specs=in_specs, out_specs=out_specs, check_vma=False)
```

profile of v0, /device:TPU:27, one launch (start us, length us, event | category | flops | bytes accessed | tf_op | source)
XLA Modules:
  0.0 216.8 jit_solution(8070249061004828400)
XLA Ops:
  0.0 0.9 copy.25
  0.9 215.2 %while.17 = (s32[]{:T(128)}, bf16[6,8192]{1,0:T(8,128)(2,1)S(1)}, bf16[6,8192]{1,0:T(8,128)(2,1)S(1)}, pred[]{:T(512)}, s32[]{:T(128)}, /*index=5*/s32[1,512]{1,...) while((s32[]{:T(128)}, bf16[6,8192]{1,0:T(8,128)(2,1)S(1)}, ...), condition=%wide.region_3.4_spmd.clone, body=%wide.region_0.3_spmd.clone.sunk | while | flops 403412992 | bytes 24471868 | solution.py:71
  0.9 7.7 %all_gather.10 = bf16[6,32768]{1,0:T(8,128)(2,1)S(1)} all-gather(bf16[6,8192]{1,0:T(8,128)(2,1)S(1)} %get-tuple-element.351), channel_id=1, replica_groups=mesh['section'=8,'neuron'=4] {'neuron'}, dimensions={1}, use_global_device_ids=true | all-gather | bytes 491520 | tf_op jit(solution)/shard_map/while/body/eval_jaxpr/all_gather | solution.py:64
  8.6 1.4 collective-permute-start
  10.1 5.5 %collective-permute-done = bf16[6,8192]{1,0:T(8,128)(2,1)S(1)} collective-permute-done((bf16[6,8192]{1,0:T(8,128)(2,1)S(1)}, bf16[6,8192]{1,0:T(8,128)(2,1)S(1)}, u32[]{:S(2)}, u32[]{:S(2)}) %collective-permute-start) | collective-permute-done | bytes 98336 | tf_op jit(solution)/shard_map/while/body/eval_jaxpr/ppermute | solution.py:13
  15.7 7.6 %all_gather.10 = bf16[6,32768]{1,0:T(8,128)(2,1)S(1)} all-gather(bf16[6,8192]{1,0:T(8,128)(2,1)S(1)} %get-tuple-element.351), channel_id=1, replica_groups=mesh['section'=8,'neuron'=4] {'neuron'}, dimensions={1}, use_global_device_ids=true | all-gather | bytes 491520 | tf_op jit(solution)/shard_map/while/body/eval_jaxpr/all_gather | solution.py:64
  23.3 1.4 collective-permute-start
  24.8 5.5 %collective-permute-done = bf16[6,8192]{1,0:T(8,128)(2,1)S(1)} collective-permute-done((bf16[6,8192]{1,0:T(8,128)(2,1)S(1)}, bf16[6,8192]{1,0:T(8,128)(2,1)S(1)}, u32[]{:S(2)}, u32[]{:S(2)}) %collective-permute-start) | collective-permute-done | bytes 98336 | tf_op jit(solution)/shard_map/while/body/eval_jaxpr/ppermute | solution.py:13
  30.3 7.4 %all_gather.10 = bf16[6,32768]{1,0:T(8,128)(2,1)S(1)} all-gather(bf16[6,8192]{1,0:T(8,128)(2,1)S(1)} %get-tuple-element.351), channel_id=1, replica_groups=mesh['section'=8,'neuron'=4] {'neuron'}, dimensions={1}, use_global_device_ids=true | all-gather | bytes 491520 | tf_op jit(solution)/shard_map/while/body/eval_jaxpr/all_gather | solution.py:64
  37.7 1.4 collective-permute-start
  39.2 6.3 %collective-permute-done = bf16[6,8192]{1,0:T(8,128)(2,1)S(1)} collective-permute-done((bf16[6,8192]{1,0:T(8,128)(2,1)S(1)}, bf16[6,8192]{1,0:T(8,128)(2,1)S(1)}, u32[]{:S(2)}, u32[]{:S(2)}) %collective-permute-start) | collective-permute-done | bytes 98336 | tf_op jit(solution)/shard_map/while/body/eval_jaxpr/ppermute | solution.py:13
  45.6 7.4 %all_gather.10 = bf16[6,32768]{1,0:T(8,128)(2,1)S(1)} all-gather(bf16[6,8192]{1,0:T(8,128)(2,1)S(1)} %get-tuple-element.351), channel_id=1, replica_groups=mesh['section'=8,'neuron'=4] {'neuron'}, dimensions={1}, use_global_device_ids=true | all-gather | bytes 491520 | tf_op jit(solution)/shard_map/while/body/eval_jaxpr/all_gather | solution.py:64
  52.9 1.4 collective-permute-start
  54.5 6.6 %collective-permute-done = bf16[6,8192]{1,0:T(8,128)(2,1)S(1)} collective-permute-done((bf16[6,8192]{1,0:T(8,128)(2,1)S(1)}, bf16[6,8192]{1,0:T(8,128)(2,1)S(1)}, u32[]{:S(2)}, u32[]{:S(2)}) %collective-permute-start) | collective-permute-done | bytes 98336 | tf_op jit(solution)/shard_map/while/body/eval_jaxpr/ppermute | solution.py:13
  61.1 7.3 %all_gather.10 = bf16[6,32768]{1,0:T(8,128)(2,1)S(1)} all-gather(bf16[6,8192]{1,0:T(8,128)(2,1)S(1)} %get-tuple-element.351), channel_id=1, replica_groups=mesh['section'=8,'neuron'=4] {'neuron'}, dimensions={1}, use_global_device_ids=true | all-gather | bytes 491520 | tf_op jit(solution)/shard_map/while/body/eval_jaxpr/all_gather | solution.py:64
  68.4 1.4 collective-permute-start
  69.9 6.5 %collective-permute-done = bf16[6,8192]{1,0:T(8,128)(2,1)S(1)} collective-permute-done((bf16[6,8192]{1,0:T(8,128)(2,1)S(1)}, bf16[6,8192]{1,0:T(8,128)(2,1)S(1)}, u32[]{:S(2)}, u32[]{:S(2)}) %collective-permute-start) | collective-permute-done | bytes 98336 | tf_op jit(solution)/shard_map/while/body/eval_jaxpr/ppermute | solution.py:13
  76.5 7.4 %all_gather.10 = bf16[6,32768]{1,0:T(8,128)(2,1)S(1)} all-gather(bf16[6,8192]{1,0:T(8,128)(2,1)S(1)} %get-tuple-element.351), channel_id=1, replica_groups=mesh['section'=8,'neuron'=4] {'neuron'}, dimensions={1}, use_global_device_ids=true | all-gather | bytes 491520 | tf_op jit(solution)/shard_map/while/body/eval_jaxpr/all_gather | solution.py:64
  83.8 1.4 collective-permute-start
  85.3 6.6 %collective-permute-done = bf16[6,8192]{1,0:T(8,128)(2,1)S(1)} collective-permute-done((bf16[6,8192]{1,0:T(8,128)(2,1)S(1)}, bf16[6,8192]{1,0:T(8,128)(2,1)S(1)}, u32[]{:S(2)}, u32[]{:S(2)}) %collective-permute-start) | collective-permute-done | bytes 98336 | tf_op jit(solution)/shard_map/while/body/eval_jaxpr/ppermute | solution.py:13
  92.0 7.3 %all_gather.10 = bf16[6,32768]{1,0:T(8,128)(2,1)S(1)} all-gather(bf16[6,8192]{1,0:T(8,128)(2,1)S(1)} %get-tuple-element.351), channel_id=1, replica_groups=mesh['section'=8,'neuron'=4] {'neuron'}, dimensions={1}, use_global_device_ids=true | all-gather | bytes 491520 | tf_op jit(solution)/shard_map/while/body/eval_jaxpr/all_gather | solution.py:64
  99.3 1.4 collective-permute-start
  100.8 87.9 %collective-permute-done = bf16[6,8192]{1,0:T(8,128)(2,1)S(1)} collective-permute-done((bf16[6,8192]{1,0:T(8,128)(2,1)S(1)}, bf16[6,8192]{1,0:T(8,128)(2,1)S(1)}, u32[]{:S(2)}, u32[]{:S(2)}) %collective-permute-start) | collective-permute-done | bytes 98336 | tf_op jit(solution)/shard_map/while/body/eval_jaxpr/ppermute | solution.py:13
  188.7 7.3 %all_gather.10 = bf16[6,32768]{1,0:T(8,128)(2,1)S(1)} all-gather(bf16[6,8192]{1,0:T(8,128)(2,1)S(1)} %get-tuple-element.351), channel_id=1, replica_groups=mesh['section'=8,'neuron'=4] {'neuron'}, dimensions={1}, use_global_device_ids=true | all-gather | bytes 491520 | tf_op jit(solution)/shard_map/while/body/eval_jaxpr/all_gather | solution.py:64
  196.0 13.3 %conditional.3 = (bf16[6,8192]{1,0:T(8,128)(2,1)S(1)}) conditional(s32[]{:T(128)} %convert_element_type.20, () %tuple.46, (s32[1,512]{1,0:T(1,128)}, s32[1,1]{1,0:T(1,128)}, s32[1,512]{1,0:T(1,128)}, bf16[6,32768]{1,0:T(8,128)(2,1)S(1)}, bf16[1,512,128,128]{3,2,1,0:T(8,128)(2,1)}) %tuple.47), branch_computations={%region_1.0_spmd, %region_2.2_spmd} | conditional | flops 403265536 | bytes 22603816 | solution.py:65
  196.0 0.7 compare_select_fusion
  196.7 1.8 gather_fusion
  198.5 0.7 compare_and_fusion
  199.2 8.4 %fusion = f32[512,6,128]{2,1,0:T(8,128)S(1)} fusion(bf16[1,512,128,128]{3,2,1,0:T(8,128)(2,1)} %get-tuple-element.210, bf16[512,6,128]{2,1,0:T(8,128)(2,1)S(1)} %gather_fusion, pred[512]{0:T(512)(128)(4,1)S(1)} %compare_and_fusion), kind=kOutput, calls=%fused_computation.1 | convolution fusion | flops 101056512 | bytes 19137024 | tf_op jit(solution)/shard_map/while/body/eval_jaxpr/cond/branch_1_fun/msk,skj->msj/dot_general | solution.py:23
  208.3 0.9 fusion.14
  209.3 1.3 collective-permute-start
  210.7 5.5 %collective-permute-done = bf16[6,8192]{1,0:T(8,128)(2,1)S(1)} collective-permute-done((bf16[6,8192]{1,0:T(8,128)(2,1)S(1)}, bf16[6,8192]{1,0:T(8,128)(2,1)S(1)}, u32[]{:S(2)}, u32[]{:S(2)}) %collective-permute-start) | collective-permute-done | bytes 98336 | tf_op jit(solution)/shard_map/while/body/eval_jaxpr/ppermute | solution.py:13
  (54 shorter events, 2.2 us)
Async XLA Ops:
  8.6 7.0 %copy-start = (bf16[6,8192]{1,0:T(8,128)(2,1)S(1)}, bf16[6,8192]{1,0:T(8,128)(2,1)}, u32[]{:S(2)}) copy-start(bf16[6,8192]{1,0:T(8,128)(2,1)} %get-tuple-element.371) | copy-start | bytes 294916 | tf_op jit(solution)/shard_map/while
  8.6 7.0 %collective-permute-start = (bf16[6,8192]{1,0:T(8,128)(2,1)S(1)}, bf16[6,8192]{1,0:T(8,128)(2,1)S(1)}, u32[]{:S(2)}, u32[]{:S(2)}) collective-permute-start(bf16[6,8192]{1,0:T(8,128)(2,1)S(1)} %get-tuple-element.374), channel_id=1, source_target_pairs={{0,4},{4,8},{8,12},{12,16},{16,20},{20,24},{24,28},{1,5},{5,9},{9,... | collective-permute-start | bytes 294920 | tf_op jit(solution)/shard_map/while/body/eval_jaxpr/ppermute | solution.py:13
  23.2 7.0 %copy-start = (bf16[6,8192]{1,0:T(8,128)(2,1)S(1)}, bf16[6,8192]{1,0:T(8,128)(2,1)}, u32[]{:S(2)}) copy-start(bf16[6,8192]{1,0:T(8,128)(2,1)} %get-tuple-element.371) | copy-start | bytes 294916 | tf_op jit(solution)/shard_map/while
  23.3 7.0 %collective-permute-start = (bf16[6,8192]{1,0:T(8,128)(2,1)S(1)}, bf16[6,8192]{1,0:T(8,128)(2,1)S(1)}, u32[]{:S(2)}, u32[]{:S(2)}) collective-permute-start(bf16[6,8192]{1,0:T(8,128)(2,1)S(1)} %get-tuple-element.374), channel_id=1, source_target_pairs={{0,4},{4,8},{8,12},{12,16},{16,20},{20,24},{24,28},{1,5},{5,9},{9,... | collective-permute-start | bytes 294920 | tf_op jit(solution)/shard_map/while/body/eval_jaxpr/ppermute | solution.py:13
  37.7 7.8 %copy-start = (bf16[6,8192]{1,0:T(8,128)(2,1)S(1)}, bf16[6,8192]{1,0:T(8,128)(2,1)}, u32[]{:S(2)}) copy-start(bf16[6,8192]{1,0:T(8,128)(2,1)} %get-tuple-element.371) | copy-start | bytes 294916 | tf_op jit(solution)/shard_map/while
  37.7 7.8 %collective-permute-start = (bf16[6,8192]{1,0:T(8,128)(2,1)S(1)}, bf16[6,8192]{1,0:T(8,128)(2,1)S(1)}, u32[]{:S(2)}, u32[]{:S(2)}) collective-permute-start(bf16[6,8192]{1,0:T(8,128)(2,1)S(1)} %get-tuple-element.374), channel_id=1, source_target_pairs={{0,4},{4,8},{8,12},{12,16},{16,20},{20,24},{24,28},{1,5},{5,9},{9,... | collective-permute-start | bytes 294920 | tf_op jit(solution)/shard_map/while/body/eval_jaxpr/ppermute | solution.py:13
  52.9 8.1 %copy-start = (bf16[6,8192]{1,0:T(8,128)(2,1)S(1)}, bf16[6,8192]{1,0:T(8,128)(2,1)}, u32[]{:S(2)}) copy-start(bf16[6,8192]{1,0:T(8,128)(2,1)} %get-tuple-element.371) | copy-start | bytes 294916 | tf_op jit(solution)/shard_map/while
  52.9 8.1 %collective-permute-start = (bf16[6,8192]{1,0:T(8,128)(2,1)S(1)}, bf16[6,8192]{1,0:T(8,128)(2,1)S(1)}, u32[]{:S(2)}, u32[]{:S(2)}) collective-permute-start(bf16[6,8192]{1,0:T(8,128)(2,1)S(1)} %get-tuple-element.374), channel_id=1, source_target_pairs={{0,4},{4,8},{8,12},{12,16},{16,20},{20,24},{24,28},{1,5},{5,9},{9,... | collective-permute-start | bytes 294920 | tf_op jit(solution)/shard_map/while/body/eval_jaxpr/ppermute | solution.py:13
  68.4 8.0 %copy-start = (bf16[6,8192]{1,0:T(8,128)(2,1)S(1)}, bf16[6,8192]{1,0:T(8,128)(2,1)}, u32[]{:S(2)}) copy-start(bf16[6,8192]{1,0:T(8,128)(2,1)} %get-tuple-element.371) | copy-start | bytes 294916 | tf_op jit(solution)/shard_map/while
  68.4 8.0 %collective-permute-start = (bf16[6,8192]{1,0:T(8,128)(2,1)S(1)}, bf16[6,8192]{1,0:T(8,128)(2,1)S(1)}, u32[]{:S(2)}, u32[]{:S(2)}) collective-permute-start(bf16[6,8192]{1,0:T(8,128)(2,1)S(1)} %get-tuple-element.374), channel_id=1, source_target_pairs={{0,4},{4,8},{8,12},{12,16},{16,20},{20,24},{24,28},{1,5},{5,9},{9,... | collective-permute-start | bytes 294920 | tf_op jit(solution)/shard_map/while/body/eval_jaxpr/ppermute | solution.py:13
  83.8 8.1 %copy-start = (bf16[6,8192]{1,0:T(8,128)(2,1)S(1)}, bf16[6,8192]{1,0:T(8,128)(2,1)}, u32[]{:S(2)}) copy-start(bf16[6,8192]{1,0:T(8,128)(2,1)} %get-tuple-element.371) | copy-start | bytes 294916 | tf_op jit(solution)/shard_map/while
  83.8 8.1 %collective-permute-start = (bf16[6,8192]{1,0:T(8,128)(2,1)S(1)}, bf16[6,8192]{1,0:T(8,128)(2,1)S(1)}, u32[]{:S(2)}, u32[]{:S(2)}) collective-permute-start(bf16[6,8192]{1,0:T(8,128)(2,1)S(1)} %get-tuple-element.374), channel_id=1, source_target_pairs={{0,4},{4,8},{8,12},{12,16},{16,20},{20,24},{24,28},{1,5},{5,9},{9,... | collective-permute-start | bytes 294920 | tf_op jit(solution)/shard_map/while/body/eval_jaxpr/ppermute | solution.py:13
  99.3 89.4 %copy-start = (bf16[6,8192]{1,0:T(8,128)(2,1)S(1)}, bf16[6,8192]{1,0:T(8,128)(2,1)}, u32[]{:S(2)}) copy-start(bf16[6,8192]{1,0:T(8,128)(2,1)} %get-tuple-element.371) | copy-start | bytes 294916 | tf_op jit(solution)/shard_map/while
  99.3 89.4 %collective-permute-start = (bf16[6,8192]{1,0:T(8,128)(2,1)S(1)}, bf16[6,8192]{1,0:T(8,128)(2,1)S(1)}, u32[]{:S(2)}, u32[]{:S(2)}) collective-permute-start(bf16[6,8192]{1,0:T(8,128)(2,1)S(1)} %get-tuple-element.374), channel_id=1, source_target_pairs={{0,4},{4,8},{8,12},{12,16},{16,20},{20,24},{24,28},{1,5},{5,9},{9,... | collective-permute-start | bytes 294920 | tf_op jit(solution)/shard_map/while/body/eval_jaxpr/ppermute | solution.py:13
  196.0 20.1 %copy-start = (bf16[6,8192]{1,0:T(8,128)(2,1)S(1)}, bf16[6,8192]{1,0:T(8,128)(2,1)}, u32[]{:S(2)}) copy-start(bf16[6,8192]{1,0:T(8,128)(2,1)} %get-tuple-element.371) | copy-start | bytes 294916 | tf_op jit(solution)/shard_map/while
  199.2 9.1 %copy-start.2 = (s32[1,512]{1,0:T(1,128)S(1)}, s32[1,512]{1,0:T(1,128)}, u32[]{:S(2)}) copy-start(s32[1,512]{1,0:T(1,128)} %get-tuple-element.206) | copy-start | bytes 6148 | tf_op jit(solution)/shard_map/while/body/eval_jaxpr/cond
  209.3 6.8 %collective-permute-start = (bf16[6,8192]{1,0:T(8,128)(2,1)S(1)}, bf16[6,8192]{1,0:T(8,128)(2,1)S(1)}, u32[]{:S(2)}, u32[]{:S(2)}) collective-permute-start(bf16[6,8192]{1,0:T(8,128)(2,1)S(1)} %get-tuple-element.374), channel_id=1, source_target_pairs={{0,4},{4,8},{8,12},{12,16},{16,20},{20,24},{24,28},{1,5},{5,9},{9,... | collective-permute-start | bytes 294920 | tf_op jit(solution)/shard_map/while/body/eval_jaxpr/ppermute | solution.py:13
  216.2 0.7 copy-start.1
where the time goes:
time: 218 us; the launch traced here: 217 us
  waiting for transfers between devices  130 us (60%)
  blocking collectives  59.3 us (27%)
  starting transfers between devices  11.3 us (5%)
  matrix products  9.28 us (4%)
  local copies, waits for them, and re-layouts  3.54 us (2%)
  other arithmetic  2.68 us (1%)
    ppermute x8, waiting for transfers between devices, from_behind(): return lax.ppermute(block, axis, route)  130 us
    all_gather x8, blocking collectives, advance(): gathered = lax.all_gather(current_in, 'neuron', axis=1, tiled=True)  59.3 us
    ppermute x8, starting transfers between devices, from_behind(): return lax.ppermute(block, axis, route)  11.3 us
    dot_general x1, matrix products, layer_apply(): jnp.einsum('msk,skj->msj', picked, weight_tiles[0], preferred_element_typ...  8.43 us
  transfers between devices with their start and end apart: 8, of which 8 were waited for; matrix products, arithmetic and copies ran while one was open for 0% of the time, Pallas kernels for 0%

commit v1 on v0

v1 whole, which is shorter than its diff:
```python
import functools

import jax
import jax.numpy as jnp
from jax import lax
from jax.experimental import pallas as pl
from jax.experimental.pallas import tpu as pltpu
from jax.sharding import PartitionSpec as P

NEURON_BIAS = -0.3
CLIP_LEVEL = 32.0
CHUNKS = 3
WCHUNKS = 8
PAD = 8
MESH = pl.DeviceIdType.MESH


def kernel(sections, shards, src_ref, live_ref, tgt_ref, in_ref, w_ref, out_ref,
           wbuf, ybuf, xbuf, pbuf, wsem, sx, rx, sy, ry, ss, rs):
    rows, cols, block = in_ref.shape
    slots = wbuf.shape[0]
    chips = shards // 2
    per = rows // CHUNKS
    wper = slots // WCHUNKS
    pstride = slots + PAD
    s = lax.axis_index("section")
    n = lax.axis_index("neuron")
    y = lax.div(n, 2)
    core = lax.rem(n, 2)
    sibling = n + 1 - 2 * core

    def peer(d):
        return lax.rem(y + d, chips) * 2 + core

    def origin(d):
        return lax.rem(y + chips - d, chips) * 2

    loads = [
        pltpu.make_async_copy(
            w_ref.at[0, pl.ds(k * wper, wper)], wbuf.at[pl.ds(k * wper, wper)], wsem.at[k]
        )
        for k in range(WCHUNKS)
    ]
    for load in loads:
        load.start()

    barrier = pltpu.get_barrier_semaphore()
    pl.semaphore_signal(barrier, inc=1, device_id=(s, sibling), device_id_type=MESH)
    for d in range(1, chips):
        pl.semaphore_signal(barrier, inc=1, device_id=(s, peer(d)), device_id_type=MESH)

    @pl.when(s > 0)
    def _():
        pl.semaphore_signal(barrier, inc=1, device_id=(s - 1, n), device_id_type=MESH)

    @pl.when(s < sections - 1)
    def _():
        pl.semaphore_signal(barrier, inc=1, device_id=(s + 1, n), device_id_type=MESH)

    pl.semaphore_wait(
        barrier,
        chips + (s > 0).astype(jnp.int32) + (s < sections - 1).astype(jnp.int32),
    )

    def at_chunk(shard, k):
        return ybuf.at[shard, pl.ds(k * per, per)]

    def along(k):
        return pltpu.make_async_remote_copy(
            src_ref=out_ref.at[pl.ds(k * per, per)], dst_ref=at_chunk(n, k),
            send_sem=sx.at[k], recv_sem=rx.at[k],
            device_id=(s + 1, n), device_id_type=MESH)

    def across(d, k):
        return pltpu.make_async_remote_copy(
            src_ref=at_chunk(n, k), dst_ref=at_chunk(n, k),
            send_sem=sy.at[d - 1, k], recv_sem=ry.at[d - 1, k],
            device_id=(s, peer(d)), device_id_type=MESH)

    def beside(d, k):
        shard = origin(d) + core
        return pltpu.make_async_remote_copy(
            src_ref=at_chunk(shard, k), dst_ref=at_chunk(shard, k),
            send_sem=ss.at[d, k], recv_sem=rs.at[d, k],
            device_id=(s, sibling), device_id_type=MESH)

    def spread(shard, k):
        for i in range(per):
            r = k * per + i
            value = ybuf[shard, r].astype(jnp.float32)
            xbuf[pl.ds(shard * cols, cols), r, :] = value

    xbuf[...] = jnp.zeros_like(xbuf)
    column = lax.broadcasted_iota(jnp.int32, (cols, slots), 0)
    place = lax.broadcasted_iota(jnp.int32, (cols, slots), 1)
    chosen = (tgt_ref[...] == column) & (place < live_ref[0, 0])
    selector = chosen.astype(jnp.float32).astype(jnp.bfloat16)

    @pl.when(s == 0)
    def _():
        ybuf[n] = in_ref[...]

    for k in range(CHUNKS):
        @pl.when(s > 0)
        def _():
            along(k).wait_recv()

        for d in range(1, chips):
            across(d, k).start()
        beside(0, k).start()
        spread(n, k)
    for k in range(CHUNKS):
        for d in range(1, chips):
            across(d, k).wait_recv()
            beside(d, k).start()
            spread(origin(d) + core, k)
    for k in range(CHUNKS):
        for d in range(chips):
            beside(d, k).wait_recv()
            spread(origin(d) + 1 - core, k)

    blank = jnp.zeros((8, block), jnp.float32)

    def multiply(t):
        j = t * 4
        x = [xbuf[src_ref[0, j + i]] for i in range(4)]
        left = jnp.concatenate([
            jnp.concatenate([x[0], blank], axis=1),
            jnp.concatenate([blank, x[1]], axis=1),
            jnp.concatenate([x[2], blank], axis=1),
            jnp.concatenate([blank, x[3]], axis=1),
        ], axis=0).astype(jnp.bfloat16)
        w = [wbuf[j + i] for i in range(4)]
        right = jnp.concatenate([
            jnp.concatenate([w[0], w[2]], axis=1),
            jnp.concatenate([w[1], w[3]], axis=1),
        ], axis=0)
        product = jnp.dot(left, right, preferred_element_type=jnp.float32)
        for i in range(4):
            half = (i // 2) * block
            pbuf[pl.ds(j + i, 8, stride=pstride), :] = product[i * 8:i * 8 + 8, half:half + block]

    for k in range(WCHUNKS):
        loads[k].wait()

        @pl.loop(0, wper // 4, unroll=4)
        def _(t):
            multiply(k * (wper // 4) + t)

    for k in range(CHUNKS):
        for i in range(per):
            r = k * per + i
            part = pbuf[r * pstride:r * pstride + slots, :]
            high = part.astype(jnp.bfloat16)
            low = (part - high.astype(jnp.float32)).astype(jnp.bfloat16)
            both = jnp.dot(
                selector, jnp.concatenate([high, low], axis=1),
                preferred_element_type=jnp.float32)
            total = both[:, :block] + both[:, block:]
            out_ref[r] = jnp.clip(total + NEURON_BIAS, 0.0, CLIP_LEVEL).astype(jnp.bfloat16)

        @pl.when(s < sections - 1)
        def _():
            along(k).start()

    for k in range(CHUNKS):
        for d in range(1, chips):
            across(d, k).wait_send()
        for d in range(chips):
            beside(d, k).wait_send()

        @pl.when(s < sections - 1)
        def _():
            along(k).wait_send()


def local(sections, shards, inputs, weight_tiles, source_block, target_block, live_slots):
    rows, width = inputs.shape
    slots, block = weight_tiles.shape[1], weight_tiles.shape[2]
    cols = width // block
    chips = shards // 2
    result = pl.pallas_call(
        functools.partial(kernel, sections, shards),
        out_shape=jax.ShapeDtypeStruct((rows, cols, block), jnp.bfloat16),
        in_specs=[
            pl.BlockSpec(memory_space=pltpu.SMEM),
            pl.BlockSpec(memory_space=pltpu.SMEM),
            pl.BlockSpec(memory_space=pltpu.VMEM),
            pl.BlockSpec(memory_space=pltpu.VMEM),
            pl.BlockSpec(memory_space=pl.ANY),
        ],
        out_specs=pl.BlockSpec(memory_space=pltpu.VMEM),
        scratch_shapes=[
            pltpu.VMEM((slots, block, block), jnp.bfloat16),
            pltpu.VMEM((shards, rows, cols, block), jnp.bfloat16),
            pltpu.VMEM((shards * cols, 8, block), jnp.float32),
            pltpu.VMEM((8 * (slots + PAD), block), jnp.float32),
            pltpu.SemaphoreType.DMA((WCHUNKS,)),
            pltpu.SemaphoreType.DMA((CHUNKS,)),
            pltpu.SemaphoreType.DMA((CHUNKS,)),
            pltpu.SemaphoreType.DMA((max(chips - 1, 1), CHUNKS)),
            pltpu.SemaphoreType.DMA((max(chips - 1, 1), CHUNKS)),
            pltpu.SemaphoreType.DMA((chips, CHUNKS)),
            pltpu.SemaphoreType.DMA((chips, CHUNKS)),
        ],
        compiler_params=pltpu.CompilerParams(
            collective_id=0, has_side_effects=True, vmem_limit_bytes=48 * 1024 * 1024),
    )(source_block, live_slots, target_block, inputs.reshape(rows, cols, block), weight_tiles)
    return result.reshape(1, rows, width)


def solution(mesh):
    in_specs = (
        P(None, "neuron"),
        P("section", "neuron", None, None),
        P("section", "neuron"),
        P("section", "neuron"),
        P("section", "neuron"),
    )
    out_specs = P("section", None, "neuron")
    body = functools.partial(local, mesh.shape["section"], mesh.shape["neuron"])
    return jax.shard_map(body, mesh=mesh, in_specs=in_specs, out_specs=out_specs, check_vma=False)
```

time: 218 us -> 117 us (0.54)
  waiting for transfers between devices: 130 us -> 0 us
  Pallas kernels: 0 us -> 113 us
  blocking collectives: 59.3 us -> 0 us
  starting transfers between devices: 11.3 us -> 0 us
  matrix products: 9.28 us -> 0 us
  other arithmetic: 2.68 us -> 0 us
    ppermute x8 -> x0, waiting for transfers between devices: 130 us -> none  [from_behind(): return lax.ppermute(block, axis, route)]
    pallas_call x0 -> x1, Pallas kernels: none -> 113 us  [local(): pl.pallas_call(functools.partial(kernel, sections, shards), out_shape=jax...]
    all_gather x8 -> x0, blocking collectives: 59.3 us -> none  [advance(): gathered = lax.all_gather(current_in, 'neuron', axis=1, tiled=True)]
    ppermute x8 -> x0, starting transfers between devices: 11.3 us -> none  [from_behind(): return lax.ppermute(block, axis, route)]
    dot_general x2 -> x0, matrix products: 9.28 us -> none  [the longest x1 8.43 us: layer_apply(): jnp.einsum('msk,skj->msj', picked, weight_tiles[0], preferred_element_typ...]
  transfers between devices with their start and end apart: 8 -> 0, of which waited for: 8 -> 0; matrix products, arithmetic and copies ran while one was open for 0% -> 0% of each run, Pallas kernels for 0% -> 0%
where the time goes in v1:
time: 117 us
  Pallas kernels  113 us (97%)
  local copies, waits for them, and re-layouts  3.06 us (3%)
    pallas_call x1, Pallas kernels, local(): pl.pallas_call(functools.partial(kernel, sections, shards), out_shape=jax...  113 us

profile of v1, /device:TPU:27, one launch (start us, length us, event | category | flops | bytes accessed | tf_op | source)
XLA Modules:
  0.0 117.0 jit_solution(8061776087468403498)
XLA Ops:
  0.7 0.9 copy.8
  1.6 0.0 copy-start
  1.6 0.7 copy-done
  2.3 0.0 copy-start.1
  2.3 0.7 copy-done.1
  2.9 113.2 %shard_map.55 = bf16[6,64,128]{2,1,0:T(8,128)(2,1)S(1)} custom-call(s32[1,512]{1,0:T(1,128)S(1)} %copy-done, s32[1,1]{1,0:T(1,128)S(6)} %copy.9.live_ref, s32[1,512]{1,0:T(1,128)S(1)} %copy-done.1, bf16[6,64,128]{2,1,0:T(8,128)(2,1)S(1)} %bitcast.4, bf16[1,512,128,128]{3,2,1,0:T(8,128)(2,1)} %w_ref.1), custom_call_target="tpu_custom_call" | custom-call | tf_op jit(solution)/shard_map/pallas_call | solution.py:182
  116.2 0.8 reshape.7
Async XLA Ops:
  1.6 0.7 copy-start
  2.3 0.7 copy-start.1

commit v2 on v1

--- a/solution.py
+++ b/solution.py
@@ -10,13 +10,14 @@
 NEURON_BIAS = -0.3
 CLIP_LEVEL = 32.0
 CHUNKS = 3
-WCHUNKS = 8
+WCHUNKS = 4
+UNROLL = 64
 PAD = 8
 MESH = pl.DeviceIdType.MESH
 
 
 def kernel(sections, shards, src_ref, live_ref, tgt_ref, in_ref, w_ref, out_ref,
-           wbuf, ybuf, xbuf, pbuf, wsem, sx, rx, sy, ry, ss, rs):
+           wbuf, ybuf, xbuf, pbuf, wsem, sx, rx, sy, ss, rs):
     rows, cols, block = in_ref.shape
     slots = wbuf.shape[0]
     chips = shards // 2
@@ -46,35 +47,39 @@
 
     barrier = pltpu.get_barrier_semaphore()
     pl.semaphore_signal(barrier, inc=1, device_id=(s, sibling), device_id_type=MESH)
-    for d in range(1, chips):
-        pl.semaphore_signal(barrier, inc=1, device_id=(s, peer(d)), device_id_type=MESH)
+
+    @pl.when(s == 0)
+    def _():
+        for d in range(1, chips):
+            pl.semaphore_signal(barrier, inc=1, device_id=(s, peer(d)), device_id_type=MESH)
 
     @pl.when(s > 0)
     def _():
-        pl.semaphore_signal(barrier, inc=1, device_id=(s - 1, n), device_id_type=MESH)
+        for d in range(chips):
+            pl.semaphore_signal(barrier, inc=1, device_id=(s - 1, peer(d)), device_id_type=MESH)
 
     @pl.when(s < sections - 1)
     def _():
-        pl.semaphore_signal(barrier, inc=1, device_id=(s + 1, n), device_id_type=MESH)
-
-    pl.semaphore_wait(
-        barrier,
-        chips + (s > 0).astype(jnp.int32) + (s < sections - 1).astype(jnp.int32),
-    )
+        for d in range(chips):
+            pl.semaphore_signal(barrier, inc=1, device_id=(s + 1, peer(d)), device_id_type=MESH)
+
+    first = (s == 0).astype(jnp.int32)
+    last = (s == sections - 1).astype(jnp.int32)
+    pl.semaphore_wait(barrier, 1 + 2 * chips - first - last * chips)
 
     def at_chunk(shard, k):
         return ybuf.at[shard, pl.ds(k * per, per)]
 
-    def along(k):
+    def along(d, k):
         return pltpu.make_async_remote_copy(
             src_ref=out_ref.at[pl.ds(k * per, per)], dst_ref=at_chunk(n, k),
-            send_sem=sx.at[k], recv_sem=rx.at[k],
-            device_id=(s + 1, n), device_id_type=MESH)
+            send_sem=sx.at[d, k], recv_sem=rx.at[d, k],
+            device_id=(s + 1, peer(d)), device_id_type=MESH)
 
     def across(d, k):
         return pltpu.make_async_remote_copy(
-            src_ref=at_chunk(n, k), dst_ref=at_chunk(n, k),
-            send_sem=sy.at[d - 1, k], recv_sem=ry.at[d - 1, k],
+            src_ref=in_ref.at[pl.ds(k * per, per)], dst_ref=at_chunk(n, k),
+            send_sem=sy.at[d, k], recv_sem=rx.at[d, k],
             device_id=(s, peer(d)), device_id_type=MESH)
 
     def beside(d, k):
@@ -98,21 +103,21 @@
 
     @pl.when(s == 0)
     def _():
+        for k in range(CHUNKS):
+            for d in range(1, chips):
+                across(d, k).start()
         ybuf[n] = in_ref[...]
 
     for k in range(CHUNKS):
         @pl.when(s > 0)
         def _():
-            along(k).wait_recv()
-
+            along(0, k).wait_recv()
+
+        beside(0, k).start()
         for d in range(1, chips):
-            across(d, k).start()
-        beside(0, k).start()
-        spread(n, k)
-    for k in range(CHUNKS):
-        for d in range(1, chips):
-            across(d, k).wait_recv()
+            along(d, k).wait_recv()
             beside(d, k).start()
+        for d in range(chips):
             spread(origin(d) + core, k)
     for k in range(CHUNKS):
         for d in range(chips):
@@ -140,12 +145,12 @@
             half = (i // 2) * block
             pbuf[pl.ds(j + i, 8, stride=pstride), :] = product[i * 8:i * 8 + 8, half:half + block]
 
-    for k in range(WCHUNKS):
-        loads[k].wait()
-
-        @pl.loop(0, wper // 4, unroll=4)
-        def _(t):
-            multiply(k * (wper // 4) + t)
+    for load in loads:
+        load.wait()
+
+    @pl.loop(0, slots // 4, unroll=min(UNROLL, slots // 4))
+    def _(t):
+        multiply(t)
 
     for k in range(CHUNKS):
         for i in range(per):
@@ -161,17 +166,23 @@
 
         @pl.when(s < sections - 1)
         def _():
-            along(k).start()
-
-    for k in range(CHUNKS):
-        for d in range(1, chips):
-            across(d, k).wait_send()
+            for d in range(chips):
+                along(d, k).start()
+
+    @pl.when(s == 0)
+    def _():
+        for k in range(CHUNKS):
+            for d in range(1, chips):
+                across(d, k).wait_send()
+
+    for k in range(CHUNKS):
         for d in range(chips):
             beside(d, k).wait_send()
 
         @pl.when(s < sections - 1)
         def _():
-            along(k).wait_send()
+            for d in range(chips):
+                along(d, k).wait_send()
 
 
 def local(sections, shards, inputs, weight_tiles, source_block, target_block, live_slots):
@@ -196,10 +207,9 @@
             pltpu.VMEM((shards * cols, 8, block), jnp.float32),
             pltpu.VMEM((8 * (slots + PAD), block), jnp.float32),
             pltpu.SemaphoreType.DMA((WCHUNKS,)),
-            pltpu.SemaphoreType.DMA((CHUNKS,)),
-            pltpu.SemaphoreType.DMA((CHUNKS,)),
-            pltpu.SemaphoreType.DMA((max(chips - 1, 1), CHUNKS)),
-            pltpu.SemaphoreType.DMA((max(chips - 1, 1), CHUNKS)),
+            pltpu.SemaphoreType.DMA((chips, CHUNKS)),
+            pltpu.SemaphoreType.DMA((chips, CHUNKS)),
+            pltpu.SemaphoreType.DMA((chips, CHUNKS)),
             pltpu.SemaphoreType.DMA((chips, CHUNKS)),
             pltpu.SemaphoreType.DMA((chips, CHUNKS)),
         ],

time: 117 us -> 87.7 us (0.75)
  Pallas kernels: 113 us -> 83.7 us
    pallas_call x1, Pallas kernels: 113 us -> 83.7 us  [local(): pl.pallas_call(functools.partial(kernel, sections, shards), out_shape=jax...]
where the time goes in v2:
time: 87.7 us; the launch traced here: 87.5 us
  Pallas kernels  83.7 us (95%)
  local copies, waits for them, and re-layouts  3.06 us (3%)
    pallas_call x1, Pallas kernels, local(): pl.pallas_call(functools.partial(kernel, sections, shards), out_shape=jax...  83.7 us
    unnamed x5, local copies, waits for them, and re-layouts  2.28 us

profile of v2, /device:TPU:27, one launch (start us, length us, event | category | flops | bytes accessed | tf_op | source)
XLA Modules:
  0.0 87.5 jit_solution(7220231050064281159)
XLA Ops:
  0.7 0.9 %copy.8 = bf16[1,6,64,128]{3,2,1,0:T(8,128)(2,1)S(1)} copy(bf16[1,6,64,128]{3,1,2,0:T(8,128)(2,1)} %bitcast.5) | data formatting | bytes 196608
  1.6 0.0 copy-start
  1.6 0.7 copy-done
  2.3 0.0 copy-start.1
  2.3 0.7 copy-done.1
  2.9 83.7 %shard_map.55 = bf16[6,64,128]{2,1,0:T(8,128)(2,1)S(1)} custom-call(s32[1,512]{1,0:T(1,128)S(1)} %copy-done, s32[1,1]{1,0:T(1,128)S(6)} %copy.9.live_ref, s32[1,512]{1,0:T(1,128)S(1)} %copy-done.1, bf16[6,64,128]{2,1,0:T(8,128)(2,1)S(1)} %bitcast.4, bf16[1,512,128,128]{3,2,1,0:T(8,128)(2,1)} %w_ref.1), custom_call_target="tpu_custom_call" | custom-call | tf_op jit(solution)/shard_map/pallas_call | solution.py:193
  86.7 0.8 reshape.7
Async XLA Ops:
  1.6 0.7 copy-start
  2.3 0.7 copy-start.1

commit v3 on v2

--- a/solution.py
+++ b/solution.py
@@ -9,7 +9,8 @@
 
 NEURON_BIAS = -0.3
 CLIP_LEVEL = 32.0
-CHUNKS = 3
+CHUNKS = 6
+GROUPS = 2
 WCHUNKS = 4
 UNROLL = 64
 PAD = 8
@@ -22,6 +23,8 @@
     slots = wbuf.shape[0]
     chips = shards // 2
     per = rows // CHUNKS
+    band = rows // GROUPS
+    held = CHUNKS // GROUPS
     wper = slots // WCHUNKS
     pstride = slots + PAD
     s = lax.axis_index("section")
@@ -93,7 +96,7 @@
         for i in range(per):
             r = k * per + i
             value = ybuf[shard, r].astype(jnp.float32)
-            xbuf[pl.ds(shard * cols, cols), r, :] = value
+            xbuf[pl.ds(shard * cols, cols), r % band, :] = value
 
     xbuf[...] = jnp.zeros_like(xbuf)
     column = lax.broadcasted_iota(jnp.int32, (cols, slots), 0)
@@ -108,21 +111,25 @@
                 across(d, k).start()
         ybuf[n] = in_ref[...]
 
-    for k in range(CHUNKS):
-        @pl.when(s > 0)
-        def _():
-            along(0, k).wait_recv()
-
-        beside(0, k).start()
-        for d in range(1, chips):
-            along(d, k).wait_recv()
-            beside(d, k).start()
-        for d in range(chips):
-            spread(origin(d) + core, k)
-    for k in range(CHUNKS):
-        for d in range(chips):
-            beside(d, k).wait_recv()
-            spread(origin(d) + 1 - core, k)
+    def receive(g):
+        for k in range(g * held, (g + 1) * held):
+            @pl.when(s > 0)
+            def _():
+                along(0, k).wait_recv()
+
+            beside(0, k).start()
+            for d in range(1, chips):
+                along(d, k).wait_recv()
+                beside(d, k).start()
+
+    def settle(g):
+        for k in range(g * held, (g + 1) * held):
+            for d in range(chips):
+                spread(origin(d) + core, k)
+        for k in range(g * held, (g + 1) * held):
+            for d in range(chips):
+                beside(d, k).wait_recv()
+                spread(origin(d) + 1 - core, k)
 
     blank = jnp.zeros((8, block), jnp.float32)
 
@@ -143,31 +150,42 @@
         product = jnp.dot(left, right, preferred_element_type=jnp.float32)
         for i in range(4):
             half = (i // 2) * block
-            pbuf[pl.ds(j + i, 8, stride=pstride), :] = product[i * 8:i * 8 + 8, half:half + block]
-
+            pbuf[pl.ds(j + i, band, stride=pstride), :] = product[i * 8:i * 8 + band, half:half + block]
+
+    def products():
+        @pl.loop(0, slots // 4, unroll=min(UNROLL, slots // 4))
+        def _(t):
+            multiply(t)
+
+    def finish(g):
+        for k in range(g * held, (g + 1) * held):
+            for r in range(k * per, (k + 1) * per):
+                at = (r % band) * pstride
+                part = pbuf[at:at + slots, :]
+                high = part.astype(jnp.bfloat16)
+                low = (part - high.astype(jnp.float32)).astype(jnp.bfloat16)
+                both = jnp.dot(
+                    selector, jnp.concatenate([high, low], axis=1),
+                    preferred_element_type=jnp.float32)
+                total = both[:, :block] + both[:, block:]
+                out_ref[r] = jnp.clip(total + NEURON_BIAS, 0.0, CLIP_LEVEL).astype(jnp.bfloat16)
+
+            @pl.when(s < sections - 1)
+            def _():
+                for d in range(chips):
+                    along(d, k).start()
+
+    receive(0)
+    settle(0)
     for load in loads:
         load.wait()
-
-    @pl.loop(0, slots // 4, unroll=min(UNROLL, slots // 4))
-    def _(t):
-        multiply(t)
-
-    for k in range(CHUNKS):
-        for i in range(per):
-            r = k * per + i
-            part = pbuf[r * pstride:r * pstride + slots, :]
-            high = part.astype(jnp.bfloat16)
-            low = (part - high.astype(jnp.float32)).astype(jnp.bfloat16)
-            both = jnp.dot(
-                selector, jnp.concatenate([high, low], axis=1),
-                preferred_element_type=jnp.float32)
-            total = both[:, :block] + both[:, block:]
-            out_ref[r] = jnp.clip(total + NEURON_BIAS, 0.0, CLIP_LEVEL).astype(jnp.bfloat16)
-
-        @pl.when(s < sections - 1)
-        def _():
-            for d in range(chips):
-                along(d, k).start()
+    for g in range(GROUPS):
+        products()
+        if g + 1 < GROUPS:
+            receive(g + 1)
+        finish(g)
+        if g + 1 < GROUPS:
+            settle(g + 1)
 
     @pl.when(s == 0)
     def _():

time: 87.7 us -> 76.7 us (0.87)
  Pallas kernels: 83.7 us -> 72.8 us
    pallas_call x1, Pallas kernels: 83.7 us -> 72.8 us  [local(): pl.pallas_call(functools.partial(kernel, sections, shards), out_shape=jax...]
where the time goes in v3:
time: 76.7 us; the launch traced here: 76.5 us
  Pallas kernels  72.8 us (95%)
  local copies, waits for them, and re-layouts  3.06 us (4%)
    pallas_call x1, Pallas kernels, local(): pl.pallas_call(functools.partial(kernel, sections, shards), out_shape=jax...  72.8 us
    unnamed x5, local copies, waits for them, and re-layouts  2.28 us

profile of v3, /device:TPU:27, one launch (start us, length us, event | category | flops | bytes accessed | tf_op | source)
XLA Modules:
  0.0 76.5 jit_solution(965034034193281174)
XLA Ops:
  0.7 0.9 %copy.8 = bf16[1,6,64,128]{3,2,1,0:T(8,128)(2,1)S(1)} copy(bf16[1,6,64,128]{3,1,2,0:T(8,128)(2,1)} %bitcast.5) | data formatting | bytes 196608
  1.6 0.0 copy-start
  1.6 0.7 copy-done
  2.3 0.0 copy-start.1
  2.3 0.7 copy-done.1
  2.9 72.8 %shard_map.55 = bf16[6,64,128]{2,1,0:T(8,128)(2,1)S(1)} custom-call(s32[1,512]{1,0:T(1,128)S(1)} %copy-done, s32[1,1]{1,0:T(1,128)S(6)} %copy.9.live_ref, s32[1,512]{1,0:T(1,128)S(1)} %copy-done.1, bf16[6,64,128]{2,1,0:T(8,128)(2,1)S(1)} %bitcast.4, bf16[1,512,128,128]{3,2,1,0:T(8,128)(2,1)} %w_ref.1), custom_call_target="tpu_custom_call" | custom-call | tf_op jit(solution)/shard_map/pallas_call | solution.py:211
  75.7 0.8 %reshape.7 = bf16[1,6,8192]{2,1,0:T(8,128)(2,1)} reshape(bf16[6,64,128]{2,1,0:T(8,128)(2,1)S(1)} %shard_map.55) | data formatting | bytes 196608 | tf_op jit(solution)/shard_map/reshape | solution.py:237
Async XLA Ops:
  1.6 0.7 copy-start
  2.3 0.7 copy-start.1

commit v4 on v3

--- a/solution.py
+++ b/solution.py
@@ -10,7 +10,7 @@
 NEURON_BIAS = -0.3
 CLIP_LEVEL = 32.0
 CHUNKS = 6
-GROUPS = 2
+GROUPS = 3
 WCHUNKS = 4
 UNROLL = 64
 PAD = 8
@@ -172,8 +172,9 @@
 
             @pl.when(s < sections - 1)
             def _():
-                for d in range(chips):
+                for d in range(1, chips):
                     along(d, k).start()
+                along(0, k).start()
 
     receive(0)
     settle(0)

time: 76.7 us -> 74.1 us (0.966)
  Pallas kernels: 72.8 us -> 70.1 us
    pallas_call x1, Pallas kernels: 72.8 us -> 70.1 us  [local(): pl.pallas_call(functools.partial(kernel, sections, shards), out_shape=jax...]
where the time goes in v4:
time: 74.1 us; the launch traced here: 73.8 us
  Pallas kernels  70.1 us (95%)
  local copies, waits for them, and re-layouts  3.06 us (4%)
    pallas_call x1, Pallas kernels, local(): pl.pallas_call(functools.partial(kernel, sections, shards), out_shape=jax...  70.1 us
    unnamed x5, local copies, waits for them, and re-layouts  2.28 us

profile of v4, /device:TPU:27, one launch (start us, length us, event | category | flops | bytes accessed | tf_op | source)
XLA Modules:
  0.0 73.8 jit_solution(13367914308725271485)
XLA Ops:
  0.7 0.9 %copy.8 = bf16[1,6,64,128]{3,2,1,0:T(8,128)(2,1)S(1)} copy(bf16[1,6,64,128]{3,1,2,0:T(8,128)(2,1)} %bitcast.5) | data formatting | bytes 196608
  1.6 0.0 copy-start
  1.6 0.7 copy-done
  2.3 0.0 copy-start.1
  2.3 0.7 copy-done.1
  2.9 70.1 %shard_map.55 = bf16[6,64,128]{2,1,0:T(8,128)(2,1)S(1)} custom-call(s32[1,512]{1,0:T(1,128)S(1)} %copy-done, s32[1,1]{1,0:T(1,128)S(6)} %copy.9.live_ref, s32[1,512]{1,0:T(1,128)S(1)} %copy-done.1, bf16[6,64,128]{2,1,0:T(8,128)(2,1)S(1)} %bitcast.4, bf16[1,512,128,128]{3,2,1,0:T(8,128)(2,1)} %w_ref.1), custom_call_target="tpu_custom_call" | custom-call | tf_op jit(solution)/shard_map/pallas_call | solution.py:212
  73.1 0.8 %reshape.7 = bf16[1,6,8192]{2,1,0:T(8,128)(2,1)} reshape(bf16[6,64,128]{2,1,0:T(8,128)(2,1)S(1)} %shard_map.55) | data formatting | bytes 196608 | tf_op jit(solution)/shard_map/reshape | solution.py:238
Async XLA Ops:
  1.6 0.7 copy-start
  2.3 0.7 copy-start.1
